TPU v7x, 32 devices: a whole 2x2x4 slice. The times are simulated.
32 devices in a mesh: row: 4 (over z), col: 8 (over y, x, core).
Axes of the slice: x: 2, y: 2, z: 4, core: 2. Of those that a mesh axis runs over, the one named last changes fastest.
Arguments:
- layer_input: bfloat16 [1024, 12288], P('col', 'row'), may hold values from -6 to 6
- heads_output: bfloat16 [1024, 6144], P('row', 'col'), may hold values from -6 to 6
- query_cot: bfloat16 [1024, 6144], P('row', 'col'), may hold values from -0.83984375 to 0.83984375
- keyval_cot: bfloat16 [1024, 1024], P('col'), may hold values from -0.83984375 to 0.83984375
- output_cot: bfloat16 [1024, 12288], P('col', 'row'), may hold values from -0.83984375 to 0.83984375
- query_weight: bfloat16 [12288, 6144], P('row', 'col'), may hold values from -0.0546875 to 0.0546875
- keyval_weight: bfloat16 [12288, 1024], P('row'), may hold values from -0.0546875 to 0.0546875
- out_weight: bfloat16 [6144, 12288], P('col', 'row'), may hold values from -0.078125 to 0.078125
Outputs:
- input_grad: bfloat16 [1024, 12288], P('col', 'row')
- heads_grad: bfloat16 [1024, 6144], P('row', 'col')
- query_wgrad: bfloat16 [12288, 6144], P('row', 'col')
- keyval_wgrad: bfloat16 [12288, 1024], P('row')
- out_wgrad: bfloat16 [6144, 12288], P('col', 'row')
All inputs are finite; a program needn't handle non-finite values.
Results may differ from a plain program's by a relative error of at most 0.001.
Values may be sent and summed in bfloat16 or wider, within the bound.
A program may use at most 192 MiB of HBM per device.

v0:
```python
import jax
import jax.numpy as jnp
from jax import lax
from jax.sharding import PartitionSpec as P


def contract_last(left, right):
    return lax.dot_general(
        left, right, (((1,), (1,)), ((), ())), preferred_element_type=jnp.float32
    )


def contract_first(left, right):
    return lax.dot_general(
        left, right, (((0,), (0,)), ((), ())), preferred_element_type=jnp.float32
    )


def shards(
    layer_input,
    heads_output,
    query_cot,
    keyval_cot,
    output_cot,
    query_weight,
    keyval_weight,
    out_weight,
):
    query_all, heads_all = (
        lax.all_gather(query_cot, "row", axis=0, tiled=True),
        lax.all_gather(heads_output, "row", axis=0, tiled=True),
    )
    output_all, input_all = (
        lax.all_gather(output_cot, "col", axis=0, tiled=True),
        lax.all_gather(layer_input, "col", axis=0, tiled=True),
    )
    keyval_term = contract_last(keyval_cot, keyval_weight)
    picked = query_all
    summed = (
        lax.psum_scatter(
            contract_last(picked, query_weight), "col", scatter_dimension=0, tiled=True
        )
        + keyval_term
    )
    input_grad = summed.astype(jnp.bfloat16)
    picked = output_all
    heads_sum = lax.psum_scatter(
        contract_last(picked, out_weight), "row", scatter_dimension=0, tiled=True
    )
    heads_grad = heads_sum.astype(jnp.bfloat16)
    query_wgrad = contract_first(input_all, query_all).astype(jnp.bfloat16)
    out_wgrad = contract_first(heads_all, output_all).astype(jnp.bfloat16)
    partial_grad = contract_first(layer_input, keyval_cot)
    keyval_wgrad = lax.psum(partial_grad, "col").astype(jnp.bfloat16)
    return (input_grad, heads_grad, query_wgrad, keyval_wgrad, out_wgrad)


def solution(mesh):
    in_specs = (
        P("col", "row"),
        P("row", "col"),
        P("row", "col"),
        P("col", None),
        P("col", "row"),
        P("row", "col"),
        P("row", None),
        P("col", "row"),
    )
    out_specs = (P("col", "row"), P("row", "col"), P("row", "col"), P("row", None), P("col", "row"))
    return jax.shard_map(shards, mesh=mesh, in_specs=in_specs, out_specs=out_specs, check_vma=False)
```

profile of v0, /device:TPU:0, one launch (start us, length us, event | category | flops | bytes accessed | tf_op | source)
XLA Modules:
  0.0 474.1 jit_solution(4525161357746585013)
XLA Ops:
  7.2 0.0 copy-start
  7.2 0.0 all-gather.7.cloned.1.call-start
  7.2 0.7 all-gather.7.cloned.1.call-update
  7.9 0.0 all-gather.5.cloned.1.call-start
  8.0 0.7 all-gather.5.cloned.1.call-update
  8.7 0.0 all-gather.11.cloned.1.call-start
  8.7 0.7 all-gather.11.cloned.1.call-update
  9.4 0.0 all-gather.9.cloned.1.call-start
  9.4 0.5 all-gather.9.cloned.1.call-update
  10.0 0.0 reduce-scatter.5.cloned.1.call-start
  10.0 48.1 %all-gather.7.cloned.1.call-done = bf16[1024,3072]{1,0:T(8,128)(2,1)} async-done(((bf16[128,3072]{1,0:T(8,128)(2,1)}), bf16[1024,3072]{1,0:T(8,128)(2,1)}) %all-gather.7.cloned.1.call-update) | async-done | bytes 6291472 | tf_op jit(solution)/shard_map/all_gather | solution.py:34
  58.2 9.7 %fusion.2 = f32[1024,768]{1,0:T(8,128)} fusion(bf16[1024,3072]{1,0:T(8,128)(2,1)} %all-gather.7.cloned.1.call-done, bf16[768,3072]{1,0:T(8,128)(2,1)} %param.15), kind=kOutput, calls=%fused_computation.5 | convolution fusion | flops 4831838208 | bytes 14155776 | tf_op jit(solution)/shard_map/dot_general | solution.py:8
  67.9 0.0 reduce-scatter.5.cloned.1.call-update
  67.9 0.0 reduce-scatter.3.cloned.1.call-start
  68.0 28.9 %all-gather.5.cloned.1.call-done = bf16[1024,768]{1,0:T(8,128)(2,1)} async-done(((bf16[256,768]{1,0:T(8,128)(2,1)}), bf16[1024,768]{1,0:T(8,128)(2,1)}) %all-gather.5.cloned.1.call-update) | async-done | bytes 1572880 | tf_op jit(solution)/shard_map/all_gather | solution.py:30
  96.9 10.0 %fusion.1 = f32[1024,3072]{1,0:T(8,128)} fusion(bf16[1024,768]{1,0:T(8,128)(2,1)} %all-gather.5.cloned.1.call-done, bf16[3072,768]{1,0:T(8,128)(2,1)} %param.13), kind=kOutput, calls=%fused_computation.4 | convolution fusion | flops 4831838208 | bytes 18874368 | tf_op jit(solution)/shard_map/dot_general | solution.py:8
  106.9 0.0 reduce-scatter.3.cloned.1.call-update
  106.9 1.1 copy-done.1
  108.0 6.3 %fusion.3 = f32[3072,1024]{1,0:T(8,128)} fusion(bf16[128,3072]{1,0:T(8,128)(2,1)S(1)} %copy-done.1, bf16[128,1024]{1,0:T(8,128)(2,1)S(1)} %copy-done), kind=kOutput, calls=%fused_computation.6 | convolution fusion | flops 805306368 | bytes 13631488 | tf_op jit(solution)/shard_map/dot_general | solution.py:14
  114.3 325.9 %all-reduce.1 = bf16[3072,1024]{1,0:T(8,128)(2,1)} all-reduce(f32[3072,1024]{1,0:T(8,128)} %fusion.3), channel_id=1, replica_groups=mesh['row'=4,'col'=8] {'col'}, use_global_device_ids=true, to_apply=%region_2.0 | all-reduce | flops 3145728 | bytes 18874368 | tf_op jit(solution)/shard_map/psum | solution.py:54
  440.2 9.2 %convolution_convert_fusion = bf16[768,3072]{1,0:T(8,128)(2,1)} fusion(bf16[1024,768]{1,0:T(8,128)(2,1)} %all-gather.11.cloned.1.call-done, bf16[1024,3072]{1,0:T(8,128)(2,1)} %all-gather.7.cloned.1.call-done), kind=kOutput, calls=%fused_computation | convolution fusion | flops 4834197504 | bytes 12582912 | tf_op jit(solution)/shard_map/dot_general | solution.py:14
  449.4 9.7 %convolution_convert_fusion.1 = bf16[3072,768]{1,0:T(8,128)(2,1)} fusion(bf16[1024,3072]{1,0:T(8,128)(2,1)} %all-gather.9.cloned.1.call-done, bf16[1024,768]{1,0:T(8,128)(2,1)S(1)} %copy-done.2), kind=kOutput, calls=%fused_computation.1 | convolution fusion | flops 4834197504 | bytes 12582912 | tf_op jit(solution)/shard_map/dot_general | solution.py:14
  459.0 1.9 convert_element_type.16
  461.0 6.3 %fusion = bf16[128,3072]{1,0:T(8,128)(2,1)} fusion(f32[128,3072]{1,0:T(8,128)} %reduce-scatter.3.cloned.1.call-done, bf16[128,1024]{1,0:T(8,128)(2,1)S(1)} %copy-done, bf16[3072,1024]{1,0:T(8,128)(2,1)} %param.14), kind=kOutput, calls=%fused_computation.3 | convolution fusion | flops 806092800 | bytes 8912896 | tf_op jit(solution)/shard_map/dot_general | solution.py:8
  (8 shorter events, 0.0 us)
Async XLA Ops:
  7.2 99.8 %copy-start = (bf16[128,1024]{1,0:T(8,128)(2,1)S(1)}, bf16[128,1024]{1,0:T(8,128)(2,1)}, u32[]{:S(2)}) copy-start(bf16[128,1024]{1,0:T(8,128)(2,1)} %param.11) | copy-start | bytes 786436
  7.2 51.0 %all-gather.7.cloned.1.call-start = ((), (), s32[]{:S(2)}) async-start(), calls=%async_computation.4 | async-start | bytes 7077888 | tf_op jit(solution)/shard_map/all_gather | solution.py:34
  7.9 88.9 %all-gather.5.cloned.1.call-start = ((), (), s32[]{:S(2)}) async-start(), calls=%async_computation.2 | async-start | bytes 1966080 | tf_op jit(solution)/shard_map/all_gather | solution.py:30
  8.7 431.5 %all-gather.11.cloned.1.call-start = ((), (), s32[]{:S(2)}) async-start(), calls=%async_computation.7 | async-start | bytes 1966080 | tf_op jit(solution)/shard_map/all_gather | solution.py:31
  9.4 440.0 %all-gather.9.cloned.1.call-start = ((), (), s32[]{:S(2)}) async-start(), calls=%async_computation.6 | async-start | bytes 7077888 | tf_op jit(solution)/shard_map/all_gather | solution.py:35
  10.0 449.1 %reduce-scatter.5.cloned.1.call-start = ((), (), s32[]{:S(2)}) async-start(), calls=%async_computation.5 | async-start | bytes 3932160 | tf_op jit(solution)/shard_map/reduce_scatter | solution.py:47
  67.9 393.0 %reduce-scatter.3.cloned.1.call-start = ((), (), s32[]{:S(2)}) async-start(), calls=%async_computation.3 | async-start | bytes 14155776 | tf_op jit(solution)/shard_map/reduce_scatter | solution.py:40
  106.9 1.1 copy-start.1
  440.2 9.2 %copy-start.2 = (bf16[1024,768]{1,0:T(8,128)(2,1)S(1)}, bf16[1024,768]{1,0:T(8,128)(2,1)}, u32[]{:S(2)}) copy-start(bf16[1024,768]{1,0:T(8,128)(2,1)} %all-gather.5.cloned.1.call-done) | copy-start | bytes 4718596
Sparse Core Ops, SparseCore 0:
  9.9 48.2 all-gather.6
  59.7 37.0 all-gather.4
  98.4 35.9 all-gather.10
  136.2 69.2 all-gather.8
  207.6 60.2 reduce-scatter.4
  271.3 142.9 reduce-scatter.2
where the time goes:
time: 474 us
  blocking collectives  326 us (69%)
  waiting for transfers between devices  79.6 us (17%)
  matrix products  51.2 us (11%)
  between operations  14.1 us (3%)
    psum x1, blocking collectives, shards(): keyval_wgrad = lax.psum(partial_grad, 'col').astype(jnp.bfloat16)  326 us
    all_gather x1, waiting for transfers between devices, shards(): lax.all_gather(output_cot, 'col', axis=0, tiled=True)  48.1 us
    all_gather x1, waiting for transfers between devices, shards(): lax.all_gather(query_cot, 'row', axis=0, tiled=True)  28.9 us
    dot_general x3, matrix products, contract_last(): lax.dot_general(left, right, (((1,), (1,)), ((), ())), preferred_element_...  26.1 us
    dot_general x3, matrix products, contract_first(): lax.dot_general(left, right, (((0,), (0,)), ((), ())), preferred_element_...  25.1 us
  transfers between devices with their start and end apart: 6, of which 2 were waited for; matrix products, arithmetic and copies ran while one was open for 10% of the time, Pallas kernels for 0%

commit v1 on v0

--- a/solution.py
+++ b/solution.py
@@ -50,8 +50,8 @@
     heads_grad = heads_sum.astype(jnp.bfloat16)
     query_wgrad = contract_first(input_all, query_all).astype(jnp.bfloat16)
     out_wgrad = contract_first(heads_all, output_all).astype(jnp.bfloat16)
-    partial_grad = contract_first(layer_input, keyval_cot)
-    keyval_wgrad = lax.psum(partial_grad, "col").astype(jnp.bfloat16)
+    keyval_all = lax.all_gather(keyval_cot, "col", axis=0, tiled=True)
+    keyval_wgrad = contract_first(input_all, keyval_all).astype(jnp.bfloat16)
     return (input_grad, heads_grad, query_wgrad, keyval_wgrad, out_wgrad)
 
 

time: 474 us -> 382 us (0.81)
  blocking collectives: 326 us -> 0 us
  waiting for transfers between devices: 79.6 us -> 309 us
  matrix products: 51.2 us -> 56 us
    psum x1 -> x0, blocking collectives: 326 us -> none  [shards(): keyval_wgrad = lax.psum(partial_grad, 'col').astype(jnp.bfloat16)]
    reduce_scatter x1, waiting for transfers between devices: 0.01 us -> 94 us  [shards(): lax.psum_scatter(contract_last(picked, query_weight), 'col', scatter_dime...]
    reduce_scatter x1, waiting for transfers between devices: 0.01 us -> 51.3 us  [shards(): lax.psum_scatter(contract_last(picked, out_weight), 'row', scatter_dimens...]
    all_gather x1, waiting for transfers between devices: 0.01 us -> 37.1 us  [shards(): lax.all_gather(layer_input, 'col', axis=0, tiled=True)]
    all_gather x1, waiting for transfers between devices: 0.01 us -> 27.5 us  [shards(): lax.all_gather(heads_output, 'row', axis=0, tiled=True)]
    all_gather x0 -> x1, waiting for transfers between devices: none -> 20 us  [shards(): keyval_all = lax.all_gather(keyval_cot, 'col', axis=0, tiled=True)]
  transfers between devices with their start and end apart: 6 -> 7, of which waited for: 2 -> 7; matrix products, arithmetic and copies ran while one was open for 10% -> 14% of each run, Pallas kernels for 0% -> 0%
where the time goes in v1:
time: 382 us
  waiting for transfers between devices  309 us (81%)
  matrix products  56 us (15%)
  between operations  14.1 us (4%)
    reduce_scatter x1, waiting for transfers between devices, shards(): lax.psum_scatter(contract_last(picked, query_weight), 'col', scatter_dime...  94 us
    reduce_scatter x1, waiting for transfers between devices, shards(): lax.psum_scatter(contract_last(picked, out_weight), 'row', scatter_dimens...  51.3 us
    all_gather x1, waiting for transfers between devices, shards(): lax.all_gather(output_cot, 'col', axis=0, tiled=True)  47.5 us
    all_gather x1, waiting for transfers between devices, shards(): lax.all_gather(layer_input, 'col', axis=0, tiled=True)  37.1 us
    dot_general x3, matrix products, contract_first(): lax.dot_general(left, right, (((0,), (0,)), ((), ())), preferred_element_...  29.9 us
    all_gather x1, waiting for transfers between devices, shards(): lax.all_gather(query_cot, 'row', axis=0, tiled=True)  28.7 us
    all_gather x1, waiting for transfers between devices, shards(): lax.all_gather(heads_output, 'row', axis=0, tiled=True)  27.5 us
    dot_general x3, matrix products, contract_last(): lax.dot_general(left, right, (((1,), (1,)), ((), ())), preferred_element_...  26.1 us
  transfers between devices with their start and end apart: 7, of which 7 were waited for; matrix products, arithmetic and copies ran while one was open for 14% of the time, Pallas kernels for 0%

profile of v1, /device:TPU:0, one launch (start us, length us, event | category | flops | bytes accessed | tf_op | source)
XLA Modules:
  0.0 381.8 jit_solution(7534110570073891354)
XLA Ops:
  7.2 0.7 all-gather.8.cloned.1.call-update
  7.9 0.0 all-gather.6.cloned.1.call-start
  7.9 0.7 all-gather.6.cloned.1.call-update
  8.6 0.0 all-gather.14.cloned.1.call-start
  8.7 0.7 all-gather.14.cloned.1.call-update
  9.4 0.0 all-gather.10.cloned.1.call-start
  9.4 0.5 all-gather.10.cloned.1.call-update
  10.0 0.5 all-gather.12.cloned.1.call-update
  10.5 0.0 reduce-scatter.5.cloned.1.call-start
  10.6 47.5 %all-gather.8.cloned.1.call-done = bf16[1024,3072]{1,0:T(8,128)(2,1)} async-done(((bf16[128,3072]{1,0:T(8,128)(2,1)}), bf16[1024,3072]{1,0:T(8,128)(2,1)}) %all-gather.8.cloned.1.call-update) | async-done | bytes 6291472 | tf_op jit(solution)/shard_map/all_gather | solution.py:34
  58.1 9.8 %fusion.2 = f32[1024,768]{1,0:T(8,128)} fusion(bf16[1024,3072]{1,0:T(8,128)(2,1)} %all-gather.8.cloned.1.call-done, bf16[768,3072]{1,0:T(8,128)(2,1)} %param.15), kind=kOutput, calls=%fused_computation.6 | convolution fusion | flops 4831838208 | bytes 14155776 | tf_op jit(solution)/shard_map/dot_general | solution.py:8
  67.9 0.2 reduce-scatter.3.cloned.1.call-start
  68.1 28.7 %all-gather.6.cloned.1.call-done = bf16[1024,768]{1,0:T(8,128)(2,1)} async-done(((bf16[256,768]{1,0:T(8,128)(2,1)}), bf16[1024,768]{1,0:T(8,128)(2,1)}) %all-gather.6.cloned.1.call-update) | async-done | bytes 1572880 | tf_op jit(solution)/shard_map/all_gather | solution.py:30
  96.8 10.0 %fusion.1 = f32[1024,3072]{1,0:T(8,128)} fusion(bf16[1024,768]{1,0:T(8,128)(2,1)} %all-gather.6.cloned.1.call-done, bf16[3072,768]{1,0:T(8,128)(2,1)} %param.13), kind=kOutput, calls=%fused_computation.5 | convolution fusion | flops 4831838208 | bytes 18874368 | tf_op jit(solution)/shard_map/dot_general | solution.py:8
  106.9 27.5 %all-gather.14.cloned.1.call-done = bf16[1024,768]{1,0:T(8,128)(2,1)} async-done(((bf16[256,768]{1,0:T(8,128)(2,1)}), bf16[1024,768]{1,0:T(8,128)(2,1)}) %all-gather.14.cloned.1.call-update) | async-done | bytes 1572880 | tf_op jit(solution)/shard_map/all_gather | solution.py:31
  134.4 9.1 %convolution_convert_fusion.1 = bf16[768,3072]{1,0:T(8,128)(2,1)} fusion(bf16[1024,768]{1,0:T(8,128)(2,1)} %all-gather.14.cloned.1.call-done, bf16[1024,3072]{1,0:T(8,128)(2,1)} %all-gather.8.cloned.1.call-done), kind=kOutput, calls=%fused_computation.1 | convolution fusion | flops 4834197504 | bytes 12582912 | tf_op jit(solution)/shard_map/dot_general | solution.py:14
  143.5 37.1 %all-gather.10.cloned.1.call-done = bf16[1024,3072]{1,0:T(8,128)(2,1)} async-done(((bf16[128,3072]{1,0:T(8,128)(2,1)}), bf16[1024,3072]{1,0:T(8,128)(2,1)}) %all-gather.10.cloned.1.call-update) | async-done | bytes 6291472 | tf_op jit(solution)/shard_map/all_gather | solution.py:35
  180.6 9.7 %convolution_convert_fusion.2 = bf16[3072,768]{1,0:T(8,128)(2,1)} fusion(bf16[1024,3072]{1,0:T(8,128)(2,1)} %all-gather.10.cloned.1.call-done, bf16[1024,768]{1,0:T(8,128)(2,1)S(1)} %copy-done.1), kind=kOutput, calls=%fused_computation.2 | convolution fusion | flops 4834197504 | bytes 12582912 | tf_op jit(solution)/shard_map/dot_general | solution.py:14
  190.2 20.0 %all-gather.12.cloned.1.call-done = bf16[1024,1024]{1,0:T(8,128)(2,1)} async-done(((bf16[128,1024]{1,0:T(8,128)(2,1)}), bf16[1024,1024]{1,0:T(8,128)(2,1)}) %all-gather.12.cloned.1.call-update) | async-done | bytes 2097168 | tf_op jit(solution)/shard_map/all_gather | solution.py:53
  210.2 11.2 %convolution_convert_fusion = bf16[3072,1024]{1,0:T(8,128)(2,1)} fusion(bf16[1024,3072]{1,0:T(8,128)(2,1)} %all-gather.10.cloned.1.call-done, bf16[1024,1024]{1,0:T(8,128)(2,1)} %all-gather.12.cloned.1.call-done), kind=kOutput, calls=%fused_computation | convolution fusion | flops 6445596672 | bytes 14680064 | tf_op jit(solution)/shard_map/dot_general | solution.py:14
  221.4 51.3 %reduce-scatter.5.cloned.1.call-done = f32[256,768]{1,0:T(8,128)} async-done(((f32[1024,768]{1,0:T(8,128)}), f32[256,768]{1,0:T(8,128)}) %reduce-scatter.5.cloned.1.call-update) | async-done | bytes 786448 | tf_op jit(solution)/shard_map/reduce_scatter | solution.py:47
  272.7 1.9 convert_element_type.16
  274.6 94.0 %reduce-scatter.3.cloned.1.call-done = f32[128,3072]{1,0:T(8,128)} async-done(((f32[1024,3072]{1,0:T(8,128)}), f32[128,3072]{1,0:T(8,128)}) %reduce-scatter.3.cloned.1.call-update) | async-done | bytes 1572880 | tf_op jit(solution)/shard_map/reduce_scatter | solution.py:40
  368.6 6.3 %fusion = bf16[128,3072]{1,0:T(8,128)(2,1)} fusion(f32[128,3072]{1,0:T(8,128)} %reduce-scatter.3.cloned.1.call-done, bf16[128,1024]{1,0:T(8,128)(2,1)S(1)} %copy-done, bf16[3072,1024]{1,0:T(8,128)(2,1)} %param.14), kind=kOutput, calls=%fused_computation.4 | convolution fusion | flops 806092800 | bytes 8912896 | tf_op jit(solution)/shard_map/dot_general | solution.py:8
  (8 shorter events, 0.1 us)
Async XLA Ops:
  7.2 51.0 %all-gather.8.cloned.1.call-start = ((), (), s32[]{:S(2)}) async-start(), calls=%async_computation.4 | async-start | bytes 7077888 | tf_op jit(solution)/shard_map/all_gather | solution.py:34
  7.9 88.9 %all-gather.6.cloned.1.call-start = ((), (), s32[]{:S(2)}) async-start(), calls=%async_computation.2 | async-start | bytes 1966080 | tf_op jit(solution)/shard_map/all_gather | solution.py:30
  8.6 125.8 %all-gather.14.cloned.1.call-start = ((), (), s32[]{:S(2)}) async-start(), calls=%async_computation.8 | async-start | bytes 1966080 | tf_op jit(solution)/shard_map/all_gather | solution.py:31
  9.4 171.2 %all-gather.10.cloned.1.call-start = ((), (), s32[]{:S(2)}) async-start(), calls=%async_computation.6 | async-start | bytes 7077888 | tf_op jit(solution)/shard_map/all_gather | solution.py:35
  10.0 200.3 %all-gather.12.cloned.1.call-start = ((), (), s32[]{:S(2)}) async-start(), calls=%async_computation.7 | async-start | bytes 2359296 | tf_op jit(solution)/shard_map/all_gather | solution.py:53
  10.5 262.1 %reduce-scatter.5.cloned.1.call-start = ((), (), s32[]{:S(2)}) async-start(), calls=%async_computation.5 | async-start | bytes 3932160 | tf_op jit(solution)/shard_map/reduce_scatter | solution.py:47
  67.9 300.7 %reduce-scatter.3.cloned.1.call-start = ((), (), s32[]{:S(2)}) async-start(), calls=%async_computation.3 | async-start | bytes 14155776 | tf_op jit(solution)/shard_map/reduce_scatter | solution.py:40
  106.9 73.7 %copy-start.1 = (bf16[1024,768]{1,0:T(8,128)(2,1)S(1)}, bf16[1024,768]{1,0:T(8,128)(2,1)}, u32[]{:S(2)}) copy-start(bf16[1024,768]{1,0:T(8,128)(2,1)} %all-gather.6.cloned.1.call-done) | copy-start | bytes 4718596
  190.2 178.4 %copy-start = (bf16[128,1024]{1,0:T(8,128)(2,1)S(1)}, bf16[128,1024]{1,0:T(8,128)(2,1)}, u32[]{:S(2)}) copy-start(bf16[128,1024]{1,0:T(8,128)(2,1)} %param.11) | copy-start | bytes 786436
Sparse Core Ops, SparseCore 0:
  9.9 48.2 all-gather.7
  59.7 37.0 all-gather.5
  98.4 35.9 all-gather.13
  136.1 44.3 all-gather.9
  182.3 27.8 all-gather.11
  212.4 60.2 reduce-scatter.4
  276.2 92.4 reduce-scatter.2

commit v2 on v1

--- a/solution.py
+++ b/solution.py
@@ -1,7 +1,13 @@
+import functools
+
 import jax
 import jax.numpy as jnp
 from jax import lax
+from jax.experimental import pallas as pl
+from jax.experimental.pallas import tpu as pltpu
 from jax.sharding import PartitionSpec as P
+
+F32, BF16 = jnp.float32, jnp.bfloat16
 
 
 def contract_last(left, right):
@@ -55,6 +61,457 @@
     return (input_grad, heads_grad, query_wgrad, keyval_wgrad, out_wgrad)
 
 
+def remote(src, dst, send, recv, device):
+    return pltpu.make_async_remote_copy(
+        src_ref=src, dst_ref=dst, send_sem=send, recv_sem=recv,
+        device_id=device, device_id_type=pl.DeviceIdType.MESH,
+    )
+
+
+CHUNKS = 6
+COPIES = 8
+
+
+class PlaneGather:
+    def __init__(self, src, whole, local, send, recv, place):
+        self.src, self.whole, self.local = src, whole, local
+        self.send, self.recv = send, recv
+        self.z, self.col, self.xn, self.yn, self.dn, self.sib, self.flip = place
+        half = src.shape[0] // 2
+        low, high = pl.ds(0, half), pl.ds(half, half)
+        w = whole
+        self.plan = [
+            (None, None, self.xn), (None, None, self.yn), (None, None, self.sib),
+            (self.xn, low, self.yn), (self.yn, high, self.xn),
+            (self.xn, None, self.sib), (self.yn, None, self.sib), (self.dn, None, self.sib),
+        ]
+        self.lands = [
+            (self.xn, None), (self.yn, None), (self.sib, None),
+            (self.dn, low), (self.dn, high),
+            (self.flip(self.xn), None), (self.flip(self.yn), None), (self.flip(self.dn), None),
+        ]
+
+    def at(self, block, rows):
+        return self.whole.at[block] if rows is None else self.whole.at[block, rows]
+
+    def copy(self, i):
+        block, rows, to = self.plan[i]
+        src = self.src if block is None else self.at(block, rows)
+        dst = self.at(self.col if block is None else block, rows)
+        return remote(src, dst, self.send.at[i], self.recv.at[i], (self.z, to))
+
+    def own(self):
+        return pltpu.make_async_copy(self.src, self.whole.at[self.col], self.local)
+
+    def arrive(self, i):
+        ref = self.at(*self.lands[i])
+        remote(ref, ref, self.send.at[i], self.recv.at[i], (self.z, self.xn)).wait_recv()
+
+    def begin(self):
+        self.own().start()
+        for i in (0, 1, 2):
+            self.copy(i).start()
+
+    def forward(self):
+        self.arrive(0)
+        self.copy(3).start()
+        self.copy(5).start()
+        self.arrive(1)
+        self.copy(4).start()
+        self.copy(6).start()
+
+    def diagonal(self):
+        self.arrive(3)
+        self.arrive(4)
+        self.copy(7).start()
+
+    def finish(self):
+        self.own().wait()
+        for i in (2, 5, 6, 7):
+            self.arrive(i)
+
+    def sent(self):
+        for i in range(COPIES):
+            self.copy(i).wait_send()
+
+
+class LineGather:
+    def __init__(self, src, whole, local, up, down, recv, z, col, n):
+        self.src, self.whole, self.local = src, whole, local
+        self.up, self.down, self.recv = up, down, recv
+        self.z, self.col, self.n = z, col, n
+
+    def copy(self, block, step, direction):
+        src = self.src if step == 0 else self.whole.at[block]
+        sems = self.up if direction > 0 else self.down
+        return remote(src, self.whole.at[block], sems.at[step], self.recv.at[block],
+                      (self.z + direction, self.col))
+
+    def own(self):
+        return pltpu.make_async_copy(self.src, self.whole.at[self.z], self.local)
+
+    def arrive(self, block):
+        ref = self.whole.at[block]
+        remote(ref, ref, self.up.at[0], self.recv.at[block], (self.z, self.col)).wait_recv()
+
+    def sends(self, k, act):
+        z, n = self.z, self.n
+
+        @pl.when((z < n - 1) & (z - k >= 0))
+        def _():
+            act(self.copy(z - k, k, 1))
+
+        @pl.when((z > 0) & (z + k <= n - 1))
+        def _():
+            act(self.copy(z + k, k, -1))
+
+    def begin(self):
+        self.own().start()
+        self.sends(0, lambda c: c.start())
+
+    def step(self, k):
+        z, n = self.z, self.n
+
+        @pl.when(z - k >= 0)
+        def _():
+            self.arrive(z - k)
+
+            @pl.when(z < n - 1)
+            def _():
+                self.copy(z - k, k, 1).start()
+
+        @pl.when(z + k <= n - 1)
+        def _():
+            self.arrive(z + k)
+
+            @pl.when(z > 0)
+            def _():
+                self.copy(z + k, k, -1).start()
+
+    def sent(self):
+        for k in range(self.n - 1):
+            self.sends(k, lambda c: c.wait_send())
+
+
+def kernel(
+    n,
+    x, ho, qc, kc, oc, qw, kw, ow,
+    ig, hg, qg, kg, og,
+    x_all, h_all, q_all, k_all, o_all, qv, kv, ov,
+    out0, sum0, in1, in2, hsum, hup, hdown, qs, ks, os,
+    local, plane_send, plane_recv, line_up, line_down, line_recv,
+    send0, recv0, send1, recv1, send2, recv2,
+    hup_send, hup_recv, hdown_send, hdown_recv, store,
+):
+    z, col = lax.axis_index("row"), lax.axis_index("col")
+    core, cx, cy = col % 2, (col // 2) % 2, col // 4
+    ox, oy, ocore = 1 - cx, 1 - cy, 1 - core
+    xn, yn = cy * 4 + ox * 2 + core, oy * 4 + cx * 2 + core
+    dn, sib = oy * 4 + ox * 2 + core, cy * 4 + cx * 2 + ocore
+
+    def flip(block):
+        return block + 1 - 2 * core
+
+    place = (z, col, xn, yn, dn, sib, flip)
+    width = qw.shape[0] // CHUNKS
+
+    loads = [pltpu.make_async_copy(a, b, local.at[5 + i])
+             for i, (a, b) in enumerate(((qw, qv), (kw, kv), (ow, ov)))]
+    for load in loads:
+        load.start()
+
+    barrier = pltpu.get_barrier_semaphore()
+    for to in (xn, yn, sib):
+        pl.semaphore_signal(barrier, inc=1, device_id=(z, to), device_id_type=pl.DeviceIdType.MESH)
+
+    @pl.when(z > 0)
+    def _():
+        pl.semaphore_signal(barrier, inc=1, device_id=(z - 1, col), device_id_type=pl.DeviceIdType.MESH)
+
+    @pl.when(z < n - 1)
+    def _():
+        pl.semaphore_signal(barrier, inc=1, device_id=(z + 1, col), device_id_type=pl.DeviceIdType.MESH)
+
+    pl.semaphore_wait(barrier, 3 + jnp.where(z > 0, 1, 0) + jnp.where(z < n - 1, 1, 0))
+
+    gx = PlaneGather(x, x_all, local.at[0], plane_send.at[0], plane_recv.at[0], place)
+    go = PlaneGather(oc, o_all, local.at[1], plane_send.at[1], plane_recv.at[1], place)
+    gk = PlaneGather(kc, k_all, local.at[2], plane_send.at[2], plane_recv.at[2], place)
+    gq = LineGather(qc, q_all, local.at[3], line_up.at[0], line_down.at[0], line_recv.at[0], z, col, n)
+    gh = LineGather(ho, h_all, local.at[4], line_up.at[1], line_down.at[1], line_recv.at[1], z, col, n)
+
+    def partial(j, which):
+        rows = q_all[:, pl.ds(which, 1)].reshape(-1, q_all.shape[-1])
+        part = contract_last(rows, qv[pl.ds(j * width, width), :])
+        return part.reshape(2, 2, -1, width)
+
+    def move0(j):
+        return remote(out0.at[j % 2], sum0.at[j], send0.at[j], recv0.at[j], (z, sib))
+
+    def move1(j):
+        if j % 2 == 0:
+            return remote(sum0.at[j, :, ox], in1.at[j], send1.at[j], recv1.at[j], (z, xn))
+        return remote(sum0.at[j, oy], in1.at[j], send1.at[j], recv1.at[j], (z, yn))
+
+    def move2(j):
+        if j % 2 == 0:
+            return remote(sum0.at[j, oy, cx], in2.at[j], send2.at[j], recv2.at[j], (z, yn))
+        return remote(sum0.at[j, cy, ox], in2.at[j], send2.at[j], recv2.at[j], (z, xn))
+
+    def stage0(j):
+        if j >= 2:
+            move0(j - 2).wait_send()
+        out0[j % 2] = partial(j, ocore)
+        move0(j).start()
+
+    def stage1(j):
+        own = partial(j, core)
+        move0(j).wait_recv()
+        sum0[j] += own
+        move1(j).start()
+
+    def stage2(j):
+        move1(j).wait_recv()
+        if j % 2 == 0:
+            sum0[j, oy, cx] += in1[j, oy]
+            move2(j).start()
+            sum0[j, cy, cx] += in1[j, cy]
+        else:
+            sum0[j, cy, ox] += in1[j, ox]
+            move2(j).start()
+            sum0[j, cy, cx] += in1[j, cx]
+
+    def stage3(j):
+        term = contract_last(k_all[col], kv[pl.ds(j * width, width), :])
+        move2(j).wait_recv()
+        total = sum0[j, cy, cx] + in2[j] + term
+        ig[:, j * width:(j + 1) * width] = total.astype(BF16)
+
+    def heads_product():
+        @pl.loop(0, n)
+        def _(b):
+            rows = o_all[pl.ds(2 * b, 2)].reshape(-1, o_all.shape[-1])
+            hsum[b] = contract_last(rows, ov[...])
+
+    def hmove(t, direction):
+        if direction > 0:
+            return remote(hsum.at[t], hup.at[t], hup_send.at[t], hup_recv.at[t], (z + 1, col))
+        return remote(hsum.at[t], hdown.at[t], hdown_send.at[t], hdown_recv.at[t], (z - 1, col))
+
+    def heads_step(p):
+        up = n - 1 - p + z
+
+        @pl.when(z <= p)
+        def _():
+            @pl.when(z > 0)
+            def _():
+                hmove(up, 1).wait_recv()
+                hsum[up] += hup[up]
+
+            hmove(up, 1).start()
+
+        down = p - (n - 1 - z)
+
+        @pl.when(n - 1 - z <= p)
+        def _():
+            @pl.when(z < n - 1)
+            def _():
+                hmove(down, -1).wait_recv()
+                hsum[down] += hdown[down]
+
+            hmove(down, -1).start()
+
+    def heads_last():
+        @pl.when(z > 0)
+        def _():
+            hmove(z, 1).wait_recv()
+            hsum[z] += hup[z]
+
+        @pl.when(z < n - 1)
+        def _():
+            hmove(z, -1).wait_recv()
+            hsum[z] += hdown[z]
+
+        hg[...] = hsum[z].astype(BF16)
+        for t in range(n):
+            @pl.when(z < t)
+            def _():
+                hmove(t, 1).wait_send()
+
+            @pl.when(z > t)
+            def _():
+                hmove(t, -1).wait_send()
+
+    tile = 256
+
+    def put(slots, slot, target, sem):
+        return pltpu.make_async_copy(slots.at[slot], target, sem.at[slot])
+
+    def layer_weights(first, last):
+        @pl.loop(first, last)
+        def _(i):
+            cols = pl.ds(pl.multiple_of(i * tile, tile), tile)
+            slot = lax.rem(i, 2)
+
+            @pl.when(i >= 2)
+            def _():
+                put(qs, slot, qg.at[cols], store.at[0]).wait()
+                put(ks, slot, kg.at[cols], store.at[1]).wait()
+
+            rows = x_all[:, :, cols].reshape(-1, tile)
+            qs[slot] = contract_first(rows, q_all[...].reshape(-1, q_all.shape[-1])).astype(BF16)
+            put(qs, slot, qg.at[cols], store.at[0]).start()
+            ks[slot] = contract_first(rows, k_all[...].reshape(-1, k_all.shape[-1])).astype(BF16)
+            put(ks, slot, kg.at[cols], store.at[1]).start()
+
+    def layer_weights_done():
+        for slot in range(2):
+            put(qs, slot, qg.at[pl.ds(0, tile)], store.at[0]).wait()
+            put(ks, slot, kg.at[pl.ds(0, tile)], store.at[1]).wait()
+
+    pieces = o_all.shape[-1] // 1024
+    out_tiles = (h_all.shape[-1] // tile) * pieces
+
+    def out_target(i):
+        cols = pl.ds(pl.multiple_of((i // pieces) * tile, tile), tile)
+        wide = pl.ds(pl.multiple_of((i % pieces) * 1024, 1024), 1024)
+        return cols, wide
+
+    def out_weights():
+        @pl.loop(0, out_tiles)
+        def _(i):
+            cols, wide = out_target(i)
+            slot = lax.rem(i, 2)
+
+            @pl.when(i >= 2)
+            def _():
+                put(os, slot, og.at[cols, wide], store.at[2]).wait()
+
+            rows = h_all[:, :, :, cols].reshape(-1, tile)
+            os[slot] = contract_first(rows, o_all[:, :, wide].reshape(-1, 1024)).astype(BF16)
+            put(os, slot, og.at[cols, wide], store.at[2]).start()
+
+        for slot in range(2):
+            put(os, slot, og.at[pl.ds(0, tile), pl.ds(0, 1024)], store.at[2]).wait()
+
+    tiles = qw.shape[0] // tile
+
+    gq.begin()
+    go.begin()
+    gk.begin()
+    gq.step(1)
+    gq.step(2)
+    gh.begin()
+    go.forward()
+    gx.begin()
+    gk.forward()
+    gq.step(3)
+    gq.own().wait()
+    for load in loads:
+        load.wait()
+    stage0(0)
+    go.diagonal()
+    gk.diagonal()
+    stage0(1)
+    stage1(0)
+    go.finish()
+    heads_product()
+    heads_step(0)
+    gh.step(1)
+    stage0(2)
+    stage1(1)
+    gk.finish()
+    gx.forward()
+    gh.step(2)
+    stage2(0)
+    stage0(3)
+    stage1(2)
+    heads_step(1)
+    gx.diagonal()
+    stage2(1)
+    stage3(0)
+    stage0(4)
+    stage1(3)
+    gh.step(3)
+    gh.own().wait()
+    stage2(2)
+    stage3(1)
+    stage0(5)
+    stage1(4)
+    stage1(5)
+    heads_step(2)
+    out_weights()
+    stage2(3)
+    stage3(2)
+    gx.finish()
+    layer_weights(0, tiles // 2)
+    stage2(4)
+    stage3(3)
+    stage2(5)
+    layer_weights(tiles // 2, tiles)
+    heads_last()
+    stage3(4)
+    stage3(5)
+    layer_weights_done()
+    for g in (gx, go, gk, gq, gh):
+        g.sent()
+    for j in range(CHUNKS):
+        if j >= CHUNKS - 2:
+            move0(j).wait_send()
+        move1(j).wait_send()
+        move2(j).wait_send()
+
+
+def fused(x, ho, qc, kc, oc, qw, kw, ow):
+    n, m = lax.axis_size("row"), lax.axis_size("col")
+    tokens, features = x.shape
+    heads, groups = qw.shape[1], kw.shape[1]
+    width = features // CHUNKS
+    split = (2, tokens, heads)
+    dma = pltpu.SemaphoreType.DMA
+    any_space = pl.BlockSpec(memory_space=pl.ANY)
+    vmem = pl.BlockSpec(memory_space=pltpu.VMEM)
+    s = jax.ShapeDtypeStruct
+    return pl.pallas_call(
+        functools.partial(kernel, n),
+        out_shape=(
+            s((tokens, features), BF16), s((2 * tokens, heads), BF16),
+            s((features, heads), BF16), s((features, groups), BF16), s((heads, features), BF16),
+        ),
+        in_specs=[any_space] * 8,
+        out_specs=(vmem, vmem, any_space, any_space, any_space),
+        scratch_shapes=[
+            pltpu.VMEM((m, tokens, features), BF16),
+            pltpu.VMEM((n,) + split, BF16),
+            pltpu.VMEM((n,) + split, BF16),
+            pltpu.VMEM((m, tokens, groups), BF16),
+            pltpu.VMEM((m, tokens, features), BF16),
+            pltpu.VMEM(qw.shape, BF16),
+            pltpu.VMEM(kw.shape, BF16),
+            pltpu.VMEM(ow.shape, BF16),
+            pltpu.VMEM((2, 2, 2, tokens, width), F32),
+            pltpu.VMEM((CHUNKS, 2, 2, tokens, width), F32),
+            pltpu.VMEM((CHUNKS, 2, tokens, width), F32),
+            pltpu.VMEM((CHUNKS, tokens, width), F32),
+            pltpu.VMEM((n, 2 * tokens, heads), F32),
+            pltpu.VMEM((n, 2 * tokens, heads), F32),
+            pltpu.VMEM((n, 2 * tokens, heads), F32),
+            pltpu.VMEM((2, 256, heads), BF16),
+            pltpu.VMEM((2, 256, groups), BF16),
+            pltpu.VMEM((2, 256, 1024), BF16),
+            dma((8,)), dma((3, COPIES)), dma((3, COPIES)),
+            dma((2, n)), dma((2, n)), dma((2, n)),
+            dma((CHUNKS,)), dma((CHUNKS,)), dma((CHUNKS,)),
+            dma((CHUNKS,)), dma((CHUNKS,)), dma((CHUNKS,)),
+            dma((n,)), dma((n,)), dma((n,)), dma((n,)), dma((3, 2)),
+        ],
+        compiler_params=pltpu.CompilerParams(
+            collective_id=0, has_side_effects=True, vmem_limit_bytes=64 * 1024 * 1024 - 65536
+        ),
+        cost_estimate=pl.CostEstimate(flops=26 * 10**9, bytes_accessed=60 * 10**6, transcendentals=0),
+    )(x, ho.reshape(split), qc.reshape(split), kc, oc, qw, kw, ow)
+
+
 def solution(mesh):
     in_specs = (
         P("col", "row"),
@@ -67,4 +524,5 @@
         P("col", "row"),
     )
     out_specs = (P("col", "row"), P("row", "col"), P("row", "col"), P("row", None), P("col", "row"))
-    return jax.shard_map(shards, mesh=mesh, in_specs=in_specs, out_specs=out_specs, check_vma=False)
+    body = fused if mesh.shape["row"] == 4 and mesh.shape["col"] == 8 else shards
+    return jax.shard_map(body, mesh=mesh, in_specs=in_specs, out_specs=out_specs, check_vma=False)

time: 382 us -> 148 us (0.39)
  waiting for transfers between devices: 309 us -> 0 us
  Pallas kernels: 0 us -> 133 us
  matrix products: 56 us -> 0 us
  local copies, waits for them, and re-layouts: 0.01 us -> 13.9 us
  between operations: 14.1 us -> 0.66 us
    all_gather x5 -> x0, waiting for transfers between devices: 161 us -> none  [the longest x1 47.5 us: shards(): lax.all_gather(output_cot, 'col', axis=0, tiled=True)]
    reduce_scatter x2 -> x0, waiting for transfers between devices: 145 us -> none  [the longest x1 94 us: shards(): lax.psum_scatter(contract_last(picked, query_weight), 'col', scatter_dime...]
    pallas_call x0 -> x1, Pallas kernels: none -> 133 us  [fused(): pl.pallas_call(functools.partial(kernel, n), out_shape=(s((tokens, featur...]
    dot_general x6 -> x0, matrix products: 56 us -> none  [the longest x3 29.9 us: contract_first(): lax.dot_general(left, right, (((0,), (0,)), ((), ())), preferred_element_...]
    unnamed x4 -> x13, local copies, waits for them, and re-layouts: 0.01 us -> 13.9 us
  transfers between devices with their start and end apart: 7 -> 0, of which waited for: 7 -> 0; matrix products, arithmetic and copies ran while one was open for 14% -> 0% of each run, Pallas kernels for 0% -> 0%
where the time goes in v2:
time: 148 us
  Pallas kernels  133 us (90%)
  local copies, waits for them, and re-layouts  13.9 us (9%)
    pallas_call x1, Pallas kernels, fused(): pl.pallas_call(functools.partial(kernel, n), out_shape=(s((tokens, featur...  133 us
    unnamed x13, local copies, waits for them, and re-layouts  13.9 us

profile of v2, /device:TPU:0, one launch (start us, length us, event | category | flops | bytes accessed | tf_op | source)
XLA Modules:
  0.0 147.6 jit_solution(1473780237223012188)
XLA Ops:
  0.6 133.0 %shard_map.119 = (bf16[128,3072]{1,0:T(8,128)(2,1)}, bf16[256,768]{1,0:T(8,128)(2,1)}, bf16[3072,768]{1,0:T(8,128)(2,1)}, bf16[3072,1024]{1,0:T(8,128)(2,1)}, bf16[768,3072]{1,0:T(8,128)(2,1)}) custom-call(bf16[128,3072]{1,0:T(8,128)(2,1)} %x.1, bf16[2,128,768]{2,1,0:T(8,128)(2,1)} %bitcast.6, bf16[2,128,768]{2,1,0:T(8,128)(2,1)} %bitcast.7, ...), custom_call_target="tpu_custom_call" | custom-call | flops 25999998976 | bytes 60000000 | tf_op jit(solution)/shard_map/pallas_call | solution.py:475
  133.7 0.0 slice-start
  133.7 2.2 %copy.18 = bf16[128,3072]{1,0:T(8,128)(2,1)} copy(bf16[128,3072]{1,0:T(8,128)(2,1)} %get-tuple-element.10) | data formatting | bytes 1572864
  135.9 1.8 %copy.19 = bf16[256,768]{1,0:T(8,128)(2,1)} copy(bf16[256,768]{1,0:T(8,128)(2,1)} %get-tuple-element.11) | data formatting | bytes 786432
  137.7 0.0 slice-start.1
  137.7 0.0 slice-start.2
  137.7 5.0 %copy.20 = bf16[3072,768]{1,0:T(8,128)(2,1)} copy(bf16[3072,768]{1,0:T(8,128)(2,1)} %get-tuple-element.12) | data formatting | bytes 9437184
  142.7 0.0 slice-done
  142.7 0.0 slice-done.1
  142.7 0.0 slice-start.3
  142.7 2.7 %copy.21 = bf16[3072,1024]{1,0:T(8,128)(2,1)} copy(bf16[3072,1024]{1,0:T(8,128)(2,1)S(1)} %bitcast.3) | data formatting | bytes 12582912
  145.4 0.0 slice-done.2
  145.4 0.0 slice-done.3
  145.4 2.2 %copy.22 = bf16[768,3072]{1,0:T(8,128)(2,1)} copy(bf16[768,3072]{1,0:T(8,128)(2,1)S(1)} %bitcast.5) | data formatting | bytes 9437184
  (2 shorter events, 0.0 us)
Async XLA Ops:
  133.7 9.0 %slice-start = ((s8[6291456]{0:T(1024)(128)(4,1)}), s8[4194304]{0:T(1024)(128)(4,1)S(1)}, s32[]{:S(2)}) async-start(s8[6291456]{0:T(1024)(128)(4,1)} %bitcast.2), calls=%async_computation | async-start | bytes 8388608
  137.7 5.0 %slice-start.1 = ((s8[6291456]{0:T(1024)(128)(4,1)}), s8[2097152]{0:T(1024)(128)(4,1)S(1)}, s32[]{:S(2)}) async-start(s8[6291456]{0:T(1024)(128)(4,1)} %bitcast.2), calls=%async_computation.1 | async-start | bytes 4194304
  137.7 7.7 %slice-start.2 = ((s8[4718592]{0:T(1024)(128)(4,1)}), s8[4194304]{0:T(1024)(128)(4,1)S(1)}, s32[]{:S(2)}) async-start(s8[4718592]{0:T(1024)(128)(4,1)} %bitcast.4), calls=%async_computation.2 | async-start | bytes 8388608
  142.7 2.7 %slice-start.3 = ((s8[4718592]{0:T(1024)(128)(4,1)}), s8[524288]{0:T(1024)(128)(4,1)S(1)}, s32[]{:S(2)}) async-start(s8[4718592]{0:T(1024)(128)(4,1)} %bitcast.4), calls=%async_computation.3 | async-start | bytes 1048576

commit v3 on v2

--- a/solution.py
+++ b/solution.py
@@ -126,7 +126,6 @@
         self.copy(7).start()
 
     def finish(self):
-        self.own().wait()
         for i in (2, 5, 6, 7):
             self.arrive(i)
 
@@ -398,20 +397,21 @@
 
     gq.begin()
     go.begin()
-    gk.begin()
     gq.step(1)
     gq.step(2)
     gh.begin()
     go.forward()
     gx.begin()
-    gk.forward()
+    gk.begin()
     gq.step(3)
     gq.own().wait()
+    go.own().wait()
+    gx.own().wait()
+    gk.own().wait()
     for load in loads:
         load.wait()
     stage0(0)
     go.diagonal()
-    gk.diagonal()
     stage0(1)
     stage1(0)
     go.finish()
@@ -420,14 +420,15 @@
     gh.step(1)
     stage0(2)
     stage1(1)
-    gk.finish()
     gx.forward()
+    gk.forward()
     gh.step(2)
     stage2(0)
     stage0(3)
     stage1(2)
     heads_step(1)
     gx.diagonal()
+    gk.diagonal()
     stage2(1)
     stage3(0)
     stage0(4)
@@ -444,6 +445,7 @@
     stage2(3)
     stage3(2)
     gx.finish()
+    gk.finish()
     layer_weights(0, tiles // 2)
     stage2(4)
     stage3(3)

time: 148 us -> 140 us (0.946); the launches traced: 148 us -> 138 us
  Pallas kernels: 133 us -> 123 us
    pallas_call x1, Pallas kernels: 133 us -> 123 us  [fused(): pl.pallas_call(functools.partial(kernel, n), out_shape=(s((tokens, featur...]
where the time goes in v3:
time: 140 us; the launch traced here: 138 us
  Pallas kernels  123 us (88%)
  local copies, waits for them, and re-layouts  13.9 us (10%)
    pallas_call x1, Pallas kernels, fused(): pl.pallas_call(functools.partial(kernel, n), out_shape=(s((tokens, featur...  123 us
    unnamed x13, local copies, waits for them, and re-layouts  13.9 us

profile of v3, /device:TPU:0, one launch (start us, length us, event | category | flops | bytes accessed | tf_op | source)
XLA Modules:
  0.0 138.0 jit_solution(13372090038647457113)
XLA Ops:
  0.6 123.5 %shard_map.119 = (bf16[128,3072]{1,0:T(8,128)(2,1)}, bf16[256,768]{1,0:T(8,128)(2,1)}, bf16[3072,768]{1,0:T(8,128)(2,1)}, bf16[3072,1024]{1,0:T(8,128)(2,1)}, bf16[768,3072]{1,0:T(8,128)(2,1)}) custom-call(bf16[128,3072]{1,0:T(8,128)(2,1)} %x.1, bf16[2,128,768]{2,1,0:T(8,128)(2,1)} %bitcast.6, bf16[2,128,768]{2,1,0:T(8,128)(2,1)} %bitcast.7, ...), custom_call_target="tpu_custom_call" | custom-call | flops 25999998976 | bytes 60000000 | tf_op jit(solution)/shard_map/pallas_call | solution.py:477
  124.1 0.0 slice-start
  124.1 2.2 %copy.18 = bf16[128,3072]{1,0:T(8,128)(2,1)} copy(bf16[128,3072]{1,0:T(8,128)(2,1)} %get-tuple-element.10) | data formatting | bytes 1572864
  126.3 1.8 %copy.19 = bf16[256,768]{1,0:T(8,128)(2,1)} copy(bf16[256,768]{1,0:T(8,128)(2,1)} %get-tuple-element.11) | data formatting | bytes 786432
  128.1 0.0 slice-start.1
  128.1 0.0 slice-start.2
  128.1 5.0 %copy.20 = bf16[3072,768]{1,0:T(8,128)(2,1)} copy(bf16[3072,768]{1,0:T(8,128)(2,1)} %get-tuple-element.12) | data formatting | bytes 9437184
  133.1 0.0 slice-done
  133.1 0.0 slice-done.1
  133.1 0.0 slice-start.3
  133.1 2.7 %copy.21 = bf16[3072,1024]{1,0:T(8,128)(2,1)} copy(bf16[3072,1024]{1,0:T(8,128)(2,1)S(1)} %bitcast.3) | data formatting | bytes 12582912
  135.8 0.0 slice-done.2
  135.8 0.0 slice-done.3
  135.8 2.2 %copy.22 = bf16[768,3072]{1,0:T(8,128)(2,1)} copy(bf16[768,3072]{1,0:T(8,128)(2,1)S(1)} %bitcast.5) | data formatting | bytes 9437184
  (2 shorter events, 0.0 us)
Async XLA Ops:
  124.1 9.0 %slice-start = ((s8[6291456]{0:T(1024)(128)(4,1)}), s8[4194304]{0:T(1024)(128)(4,1)S(1)}, s32[]{:S(2)}) async-start(s8[6291456]{0:T(1024)(128)(4,1)} %bitcast.2), calls=%async_computation | async-start | bytes 8388608
  128.1 5.0 %slice-start.1 = ((s8[6291456]{0:T(1024)(128)(4,1)}), s8[2097152]{0:T(1024)(128)(4,1)S(1)}, s32[]{:S(2)}) async-start(s8[6291456]{0:T(1024)(128)(4,1)} %bitcast.2), calls=%async_computation.1 | async-start | bytes 4194304
  128.1 7.7 %slice-start.2 = ((s8[4718592]{0:T(1024)(128)(4,1)}), s8[4194304]{0:T(1024)(128)(4,1)S(1)}, s32[]{:S(2)}) async-start(s8[4718592]{0:T(1024)(128)(4,1)} %bitcast.4), calls=%async_computation.2 | async-start | bytes 8388608
  133.1 2.7 %slice-start.3 = ((s8[4718592]{0:T(1024)(128)(4,1)}), s8[524288]{0:T(1024)(128)(4,1)S(1)}, s32[]{:S(2)}) async-start(s8[4718592]{0:T(1024)(128)(4,1)} %bitcast.4), calls=%async_computation.3 | async-start | bytes 1048576
